TPU v7x, 128 devices: a whole 4x4x4 slice. The times are simulated.
128 devices in a mesh: gx: 8 (over y, z_lo), gy: 16 (over z_hi, x, core).
Axes of the slice: x: 4, y: 4, z: 4 (z_hi: 2, z_lo: 2; z = z_hi * 2 + z_lo), core: 2. Of those that a mesh axis runs over, the one named last changes fastest.
Arguments:
- velocity: float32 [3, 96, 448, 1024], P(None, 'gx', 'gy'), may hold values from -12 to 12
- viscosity: float32 [96, 448, 1024], P('gx', 'gy'), may hold values from 0.5 to 4
- cells: int32 [3, 131072], P(None, ('gx', 'gy')), may hold values from 0 to 1023, as said below
- offsets: float32 [3, 131072], P(None, ('gx', 'gy')), may hold values from 0 to 1
- forces: float32 [3, 131072], P(None, ('gx', 'gy')), may hold values from -48 to 48
- owners: int32 [131072, 1], P(('gx', 'gy')), may hold values from 0 to 127; in each aligned block of 1024 rows (0 to 1023, 1024 to 2047, ...) at most 16 rows name the same one
Outputs:
- new_velocity: float32 [3, 96, 448, 1024], P(None, 'gx', 'gy')
- marker_velocity: float32 [3, 131072], P(None, ('gx', 'gy'))
Inputs may be any that keep to these rules, and one draw needn't show every extreme that they name: cells[0] lies below 12, cells[1] below 28, cells[2] below 1024. `owners`: among one device's 1024 markers at most 16 have the same owner, and in every draw some owner is named exactly 16 times by one device's markers.
All inputs are finite; a program needn't handle non-finite values.
Results may differ from a plain program's by a relative error of at most 0.000096.
Values sent between devices are 32-bit elements; how exact they have to be, the bound alone decides.
No kernel may reach another device: no remote copies, remote signals or barrier semaphores. Data moves between devices by JAX's collectives and lax.ppermute only.
A program may use at most 128 MiB of HBM per device.

v0:
```python
import jax
import jax.numpy as jnp
from jax import lax
from jax.sharding import PartitionSpec as P

SWEEPS = 3


def split_up(x, dim, length):
    shape = x.shape
    pieces = x.reshape(*shape[:dim], length, shape[dim] // length, *shape[dim + 1 :])
    return jnp.moveaxis(pieces, dim, 0)


def in_order(pieces, dim):
    shape = list(pieces.shape[1:])
    shape[dim] *= pieces.shape[0]
    return jnp.moveaxis(pieces, 0, dim).reshape(shape)


def joined_exchange(x, axis, axes, splits, concats):
    sizes = [lax.axis_size(a) for a in axes]
    pieces = split_up(x, splits[0], sizes[0])
    pieces = jnp.moveaxis(split_up(pieces, splits[1] + 1, sizes[1]), 0, 1)
    inside = pieces.shape[2:]
    pieces = pieces.reshape(-1, *inside)
    pieces = lax.all_to_all(pieces, axis, split_axis=0, concat_axis=0, tiled=True)
    pieces = in_order(pieces.reshape(*sizes, *inside), concats[0] + 1)
    return in_order(pieces, concats[1])


def extended(block, sides, width):
    for axis, dim in sides:
        count = lax.axis_size(axis)
        forward = [(i, i + 1) for i in range(count - 1)]
        forward.append((count - 1, 0))
        backward = [(target, source) for source, target in forward]
        low = lax.ppermute(
            lax.slice_in_dim(block, block.shape[dim] - width, None, axis=dim), axis, forward
        )
        high = lax.ppermute(lax.slice_in_dim(block, 0, width, axis=dim), axis, backward)
        block = jnp.concatenate([low, block, high], axis=dim)
    return block


def kernel_weights(frac):
    root = jnp.sqrt(1.0 + 4.0 * frac - 4.0 * frac * frac)
    return jnp.stack(
        [
            (3.0 - 2.0 * frac - root) / 8.0,
            (3.0 - 2.0 * frac + root) / 8.0,
            (1.0 + 2.0 * frac + root) / 8.0,
            (1.0 + 2.0 * frac - root) / 8.0,
        ]
    )


def tent_table(first, weights, width, periodic):
    columns = lax.broadcasted_iota(jnp.int32, (first.shape[0], width), 1)
    table = jnp.zeros((first.shape[0], width), jnp.float32)
    for j in range(4):
        target = first + j
        if periodic:
            target = jnp.mod(target, width)
        table = table + jnp.where(columns == target[:, None], weights[j][:, None], 0.0)
    return table


def block_tables(received, start, block, ext_x, ext_y, depth):
    part = lax.dynamic_slice_in_dim(received, start, block, 1)
    local_x = part[0].astype(jnp.int32)
    local_y = part[1].astype(jnp.int32)
    local_z = part[2].astype(jnp.int32)
    table_x = tent_table(local_x + 1, kernel_weights(part[3]), ext_x, False)
    table_y = tent_table(local_y + 1, kernel_weights(part[4]), ext_y, False)
    table_z = tent_table(local_z - 1, kernel_weights(part[5]), depth, True)
    planar = (table_x[:, :, None] * table_y[:, None, :]).reshape(block, ext_x * ext_y)
    return (planar, table_z, part)


def neighbour_sum(padded):
    inner = padded[:, 1:-1, 1:-1]
    beside_all = padded[:, 2:, 1:-1] + padded[:, :-2, 1:-1]
    beside_all = beside_all + padded[:, 1:-1, 2:] + padded[:, 1:-1, :-2]
    beside_all = beside_all + jnp.roll(inner, -1, 3) + jnp.roll(inner, 1, 3)
    return beside_all


def fold_axis(padded, axis, length):
    middle = lax.slice_in_dim(padded, 4, length + 4, axis=axis)
    lower = lax.slice_in_dim(padded, 0, 2, axis=axis)
    upper = lax.slice_in_dim(padded, length + 6, length + 8, axis=axis)
    head = lax.slice_in_dim(middle, 0, 2, axis=axis) + lower
    centre = lax.slice_in_dim(middle, 2, length - 2, axis=axis)
    tail = lax.slice_in_dim(middle, length - 2, length, axis=axis) + upper
    return jnp.concatenate([head, centre, tail], axis=axis)


def redistribute(payload, rows_gx, rows_gy):
    width = payload.shape[0]
    split = payload.reshape(width, rows_gx, rows_gy, -1)
    moved = joined_exchange(split, ("gx", "gy"), ("gx", "gy"), (1, 2), (1, 2))
    return moved.reshape(width, -1)


def shards(velocity, viscosity, cells, offsets, forces, owners):
    rows_gx = lax.axis_size("gx")
    rows_gy = lax.axis_size("gy")
    devices = rows_gx * rows_gy
    markers = owners.shape[0]
    capacity = max(2, 2 * markers // devices)
    slots = capacity * devices
    size_x = velocity.shape[1]
    size_y = velocity.shape[2]
    depth = velocity.shape[3]
    ext_x = size_x + 4
    ext_y = size_y + 4
    owner = owners[:, 0]
    group = min(128, markers)
    onehot = (owner[:, None] == lax.broadcasted_iota(jnp.int32, (markers, devices), 1)).astype(
        jnp.float32
    )
    onehot = onehot.reshape(markers // group, group, devices)
    lower_tri = (
        lax.broadcasted_iota(jnp.int32, (group, group), 0)
        > lax.broadcasted_iota(jnp.int32, (group, group), 1)
    ).astype(jnp.float32)
    within = jnp.einsum("ij,bjd->bid", lower_tri, onehot, precision=lax.Precision.HIGHEST)
    totals = jnp.sum(onehot, axis=1)
    before = jnp.cumsum(totals, axis=0) - totals
    rank = (
        jnp.sum((within + before[:, None, :]) * onehot, axis=-1).reshape(markers).astype(jnp.int32)
    )
    slot = owner * capacity + rank
    payload = jnp.concatenate([cells.astype(jnp.float32), offsets, forces], axis=0)
    outgoing = jnp.zeros((9, slots), jnp.float32).at[:, slot].set(payload)
    received = redistribute(outgoing, rows_gx, rows_gy)
    block = min(512, slots)
    turns = slots // block

    def spread_block(turn, spread):
        planar, table_z, part = block_tables(received, turn * block, block, ext_x, ext_y, depth)
        pushed = part[6:9][:, :, None] * table_z[None, :, :]
        return spread + jnp.einsum("sk,csz->ckz", planar, pushed, precision=lax.Precision.HIGHEST)

    spread = lax.fori_loop(
        0, turns, spread_block, jnp.zeros((3, ext_x * ext_y, depth), jnp.float32)
    )
    spread = spread.reshape(3, ext_x, ext_y, depth)
    gathered = extended(spread, (("gx", 1), ("gy", 2)), 2)
    folded = fold_axis(fold_axis(gathered, 1, size_x), 2, size_y)
    rhs = velocity + folded
    field = rhs
    for sweep in range(SWEEPS):
        padded = extended(field, (("gx", 1), ("gy", 2)), 1)
        field = (rhs + viscosity * neighbour_sum(padded)) / (1.0 + 6.0 * viscosity)
    field_ext = extended(field, (("gx", 1), ("gy", 2)), 2)
    field_flat = field_ext.reshape(3, ext_x * ext_y, depth)

    def sample_block(turn, speeds):
        planar, table_z, part = block_tables(received, turn * block, block, ext_x, ext_y, depth)
        columns = jnp.einsum("sk,ckz->csz", planar, field_flat, precision=lax.Precision.HIGHEST)
        values = jnp.sum(columns * table_z[None, :, :], axis=-1)
        return lax.dynamic_update_slice_in_dim(speeds, values, turn * block, 1)

    sampled = lax.fori_loop(0, turns, sample_block, jnp.zeros((3, slots), jnp.float32))
    returned = redistribute(sampled, rows_gx, rows_gy)
    marker_velocity = returned[:, slot]
    return (field, marker_velocity)


def solution(mesh):
    in_specs = (
        P(None, "gx", "gy", None),
        P("gx", "gy", None),
        P(None, ("gx", "gy")),
        P(None, ("gx", "gy")),
        P(None, ("gx", "gy")),
        P(("gx", "gy"), None),
    )
    out_specs = (P(None, "gx", "gy", None), P(None, ("gx", "gy")))
    return jax.shard_map(shards, mesh=mesh, in_specs=in_specs, out_specs=out_specs, check_vma=False)
```

profile of v0, /device:TPU:1, one launch (start us, length us, event | category | flops | bytes accessed | tf_op | source)
XLA Modules:
  0.0 428.4 jit_solution(15032379849644767117)
XLA Ops:
  5.0 3.3 scatter_custom_fusion
  9.8 2.1 reduce.1
  13.0 12.1 %all-to-all-start = ((f32[128,1,144]{2,1,0:T(1,128)}), f32[128,1,144]{2,1,0:T(1,128)S(1)}, u32[]{:S(2)}, u32[]{:S(2)}) async-start(f32[128,1,144]{2,1,0:T(1,128)} %reshape.1849), calls=%async_computation | async-start | bytes 262144 | tf_op jit(solution)/shard_map/all_to_all | solution.py:27
  25.2 10.1 %all-to-all-done = f32[128,1,144]{2,1,0:T(1,128)S(1)} async-done(((f32[128,1,144]{2,1,0:T(1,128)}), f32[128,1,144]{2,1,0:T(1,128)S(1)}, u32[]{:S(2)}, u32[]{:S(2)}) %all-to-all-start) | async-done | bytes 73760 | tf_op jit(solution)/shard_map/all_to_all | solution.py:27
  38.1 58.0 %while.38 = (s32[]{:T(128)}, f32[3,512,1024]{1,2,0:T(8,128)}, f32[9,2048]{1,0:T(8,128)S(1)}, s32[]{:T(128)}, s32[]{:T(128)}, /*index=5*/s32[]{}, s32[]{:T(128)}, s32[]{:T(128)}, s32[]{}, s32[]{}, /*index=10*/s32[]{}, s32[]{}, s32[]{}) while((s32[]{:T(128)}, f32[3,512,1024]{1,2,0:T(8,128)}, f32[9,2048]{1,0:T(8,128)S(1)}, s32[]{:T(128)}, ...), condition=%wide.region_5.6_spmd.clone, body=%wide.region_4.5_spmd.clone.sunk | while | flops 9674747904 | bytes 19216668 | solution.py:146
  39.6 11.8 %bitcast_add_fusion.2 = f32[3,512,1024]{1,2,0:T(8,128)} fusion(f32[3,512,1024]{1,2,0:T(8,128)} %get-tuple-element.627, pred[]{:T(512)S(6)} %compare.43, f32[512,512,1]{0,1,2:T(8,128)S(1)} %bitcast.166, f32[512,1024]{0,1:T(8,128)S(1)} %select_add_fusion.17, f32[3,512]{1,0:T(4,128)S(1)} %dynamic-slice.76), kind=kOutput, calls=%fused_computation.71.clone.1 | convolution fusion | flops 9668395008 | bytes 15734785 | tf_op jit(solution)/shard_map/while/body/eval_jaxpr/sk,csz->ckz/dot_general | solution.py:144
  52.9 13.4 %bitcast_add_fusion.2 = f32[3,512,1024]{1,2,0:T(8,128)} fusion(f32[3,512,1024]{1,2,0:T(8,128)} %get-tuple-element.627, pred[]{:T(512)S(6)} %compare.43, f32[512,512,1]{0,1,2:T(8,128)S(1)} %bitcast.166, f32[512,1024]{0,1:T(8,128)S(1)} %select_add_fusion.17, f32[3,512]{1,0:T(4,128)S(1)} %dynamic-slice.76), kind=kOutput, calls=%fused_computation.71.clone.1 | convolution fusion | flops 9668395008 | bytes 15734785 | tf_op jit(solution)/shard_map/while/body/eval_jaxpr/sk,csz->ckz/dot_general | solution.py:144
  67.8 13.4 %bitcast_add_fusion.2 = f32[3,512,1024]{1,2,0:T(8,128)} fusion(f32[3,512,1024]{1,2,0:T(8,128)} %get-tuple-element.627, pred[]{:T(512)S(6)} %compare.43, f32[512,512,1]{0,1,2:T(8,128)S(1)} %bitcast.166, f32[512,1024]{0,1:T(8,128)S(1)} %select_add_fusion.17, f32[3,512]{1,0:T(4,128)S(1)} %dynamic-slice.76), kind=kOutput, calls=%fused_computation.71.clone.1 | convolution fusion | flops 9668395008 | bytes 15734785 | tf_op jit(solution)/shard_map/while/body/eval_jaxpr/sk,csz->ckz/dot_general | solution.py:144
  82.7 13.4 %bitcast_add_fusion.2 = f32[3,512,1024]{1,2,0:T(8,128)} fusion(f32[3,512,1024]{1,2,0:T(8,128)} %get-tuple-element.627, pred[]{:T(512)S(6)} %compare.43, f32[512,512,1]{0,1,2:T(8,128)S(1)} %bitcast.166, f32[512,1024]{0,1:T(8,128)S(1)} %select_add_fusion.17, f32[3,512]{1,0:T(4,128)S(1)} %dynamic-slice.76), kind=kOutput, calls=%fused_computation.71.clone.1 | convolution fusion | flops 9668395008 | bytes 15734785 | tf_op jit(solution)/shard_map/while/body/eval_jaxpr/sk,csz->ckz/dot_general | solution.py:144
  96.1 6.6 %copy.99 = f32[3,512,1024]{2,1,0:T(8,128)} copy(f32[3,512,1024]{1,2,0:T(8,128)} %get-tuple-element.327) | data formatting | bytes 12582912 | tf_op jit(solution)/shard_map/while | solution.py:146
  104.8 3.0 collective-permute-start.1
  107.8 30.4 %collective-permute-done = f32[3,2,32,1024]{3,2,1,0:T(8,128)S(1)} collective-permute-done((f32[3,2,32,1024]{3,2,1,0:T(8,128)S(1)}, f32[3,2,32,1024]{3,2,1,0:T(8,128)S(1)}, u32[]{:S(2)}, u32[]{:S(2)}) %collective-permute-start) | collective-permute-done | bytes 786464 | tf_op jit(solution)/shard_map/ppermute | solution.py:38
  138.2 1.9 collective-permute-done.1
  140.1 2.4 pad_maximum_fusion.29
  146.2 5.1 %collective-permute-done.2 = f32[3,20,2,1024]{3,1,2,0:T(8,128)S(1)} collective-permute-done((f32[3,20,2,1024]{3,1,2,0:T(8,128)S(1)}, f32[3,20,2,1024]{3,1,2,0:T(8,128)S(1)}, u32[]{:S(2)}, u32[]{:S(2)}) %collective-permute-start.2) | collective-permute-done | bytes 491552 | tf_op jit(solution)/shard_map/ppermute | solution.py:38
  151.6 2.8 collective-permute-done.3
  154.8 1.9 pad_maximum_fusion
  160.5 3.5 maximum_add_fusion
  165.7 5.3 %fusion.68 = (f32[3,12,28,1023]{3,2,1,0:T(8,128)}, f32[3,12,28,1023]{3,2,1,0:T(8,128)}) fusion(f32[3,12,28,1024]{3,2,1,0:T(8,128)S(1)} %maximum_add_fusion), kind=kLoop, calls=%fused_computation.240 | loop fusion | bytes 16498944 | tf_op jit(solution)/shard_map/jit(_roll_static)/slice | solution.py:85
  171.0 9.9 %collective-permute-done.4 = f32[3,1,28,1024]{3,2,1,0:T(8,128)S(1)} collective-permute-done((f32[3,1,28,1024]{3,2,1,0:T(8,128)S(1)}, f32[3,1,28,1024]{3,2,1,0:T(8,128)S(1)}, u32[]{:S(2)}, u32[]{:S(2)}) %collective-permute-start.4) | collective-permute-done | bytes 344096 | tf_op jit(solution)/shard_map/ppermute | solution.py:41
  182.7 1.9 collective-permute-start.6
  189.6 11.6 %fusion.47 = f32[3,12,28,1024]{3,2,1,0:T(8,128)} fusion(f32[3,12,28,1024]{3,2,1,0:T(8,128)S(1)} %maximum_add_fusion, f32[3,14,1,1024]{3,2,1,0:T(1,128)} %copy.107, f32[3,1,28,1024]{3,2,1,0:T(8,128)S(1)} %collective-permute-done.4, f32[3,1,28,1024]{3,2,1,0:T(8,128)} %copy-done.4, f32[3,14,1,1024]{3,2,1,0:T(1,128)} %copy.105, ...), kind=kLoop, calls=%fused_computation.184 | loop fusion | flops 18579456 | bytes 20299776 | tf_op jit(solution)/shard_map/div | solution.py:156
  202.4 3.3 collective-permute-start.8
  205.8 9.1 %fusion.65 = (f32[3,12,28,1023]{3,2,1,0:T(8,128)}, f32[3,12,28,1023]{3,2,1,0:T(8,128)}) fusion(f32[3,12,28,1024]{3,2,1,0:T(8,128)} %fusion.47), kind=kLoop, calls=%fused_computation.237 | loop fusion | bytes 16498944 | tf_op jit(solution)/shard_map/jit(_roll_static)/slice | solution.py:85
  214.8 7.3 %collective-permute-done.9 = f32[3,1,28,1024]{3,2,1,0:T(8,128)S(1)} collective-permute-done((f32[3,1,28,1024]{3,2,1,0:T(8,128)S(1)}, f32[3,1,28,1024]{3,2,1,0:T(8,128)S(1)}, u32[]{:S(2)}, u32[]{:S(2)}) %collective-permute-start.9) | collective-permute-done | bytes 344096 | tf_op jit(solution)/shard_map/ppermute | solution.py:38
  225.6 2.0 collective-permute-done.10
  229.4 15.5 %fusion.39 = f32[3,12,28,1024]{3,2,1,0:T(8,128)} fusion(f32[3,12,28,1024]{3,2,1,0:T(8,128)S(1)} %maximum_add_fusion, f32[3,14,1,1024]{3,2,1,0:T(1,128)} %copy.111, f32[3,1,28,1024]{3,2,1,0:T(8,128)S(1)} %collective-permute-done.8, f32[3,12,28,1024]{3,2,1,0:T(8,128)} %fusion.47, f32[3,1,28,1024]{3,2,1,0:T(8,128)} %copy-done.3, f32[3,14,1,1024]{3,2,1,0:T(1,128)} %copy.109, ...), kind=kLoop, calls=%fused_computation.168 | loop fusion | flops 18579456 | bytes 24428544 | tf_op jit(solution)/shard_map/div | solution.py:156
  246.1 2.5 collective-permute-start.12
  249.0 9.0 %fusion.62 = (f32[3,12,28,1023]{3,2,1,0:T(8,128)}, f32[3,12,28,1023]{3,2,1,0:T(8,128)}) fusion(f32[3,12,28,1024]{3,2,1,0:T(8,128)} %fusion.39), kind=kLoop, calls=%fused_computation.234 | loop fusion | bytes 16498944 | tf_op jit(solution)/shard_map/jit(_roll_static)/slice | solution.py:85
  258.0 6.3 %collective-permute-done.13 = f32[3,1,28,1024]{3,2,1,0:T(8,128)S(1)} collective-permute-done((f32[3,1,28,1024]{3,2,1,0:T(8,128)S(1)}, f32[3,1,28,1024]{3,2,1,0:T(8,128)S(1)}, u32[]{:S(2)}, u32[]{:S(2)}) %collective-permute-start.13) | collective-permute-done | bytes 344096 | tf_op jit(solution)/shard_map/ppermute | solution.py:38
  264.7 2.6 collective-permute-start.14
  269.5 2.0 collective-permute-done.14
  273.2 15.6 %fusion.31 = f32[3,12,28,1024]{3,2,1,0:T(8,128)} fusion(f32[3,12,28,1024]{3,2,1,0:T(8,128)S(1)} %maximum_add_fusion, f32[3,14,1,1024]{3,2,1,0:T(1,128)} %copy.115, f32[3,1,28,1024]{3,2,1,0:T(8,128)S(1)} %collective-permute-done.12, f32[3,12,28,1024]{3,2,1,0:T(8,128)} %fusion.39, f32[3,1,28,1024]{3,2,1,0:T(8,128)} %copy-done.2, ...), kind=kLoop, calls=%fused_computation.152 | loop fusion | flops 18579456 | bytes 24428544 | tf_op jit(solution)/shard_map/div | solution.py:156
  290.9 2.1 collective-permute-start.16
  295.2 26.2 %collective-permute-done.16 = f32[3,2,28,1024]{3,1,2,0:T(2,128)S(1)} collective-permute-done((f32[3,2,28,1024]{3,1,2,0:T(2,128)S(1)}, f32[3,2,28,1024]{3,1,2,0:T(2,128)S(1)}, u32[]{:S(2)}, u32[]{:S(2)}) %collective-permute-start.16) | collective-permute-done | bytes 688160 | tf_op jit(solution)/shard_map/ppermute | solution.py:38
  321.6 3.6 collective-permute-done.17
  326.0 1.9 collective-permute-start.18
  328.3 4.3 %collective-permute-done.18 = f32[3,16,2,1024]{3,1,2,0:T(8,128)S(1)} collective-permute-done((f32[3,16,2,1024]{3,1,2,0:T(8,128)S(1)}, f32[3,16,2,1024]{3,1,2,0:T(8,128)S(1)}, u32[]{:S(2)}, u32[]{:S(2)}) %collective-permute-start.18) | collective-permute-done | bytes 393248 | tf_op jit(solution)/shard_map/ppermute | solution.py:38
  332.9 2.8 collective-permute-done.19
  336.1 5.1 %pad_maximum_fusion.1 = f32[3,16,32,1024]{3,2,1,0:T(8,128)} fusion(f32[3,16,2,1024]{3,2,1,0:T(2,128)S(1)} %copy.123, f32[3,2,28,1024]{3,2,1,0:T(8,128)S(1)} %copy.119, f32[3,12,28,1024]{3,2,1,0:T(8,128)} %fusion.31, f32[3,2,28,1024]{3,2,1,0:T(8,128)S(1)} %copy.118, f32[3,16,2,1024]{3,2,1,0:T(2,128)S(1)} %copy.122), kind=kLoop, calls=%fused_computation.144 | loop fusion | flops 6291456 | bytes 12582912 | tf_op jit(solution)/shard_map/concatenate | solution.py:42
  341.1 62.3 %while.37 = (s32[]{:T(128)}, f32[3,2048]{1,0:T(4,128)S(1)}, f32[9,2048]{1,0:T(8,128)}, f32[3,512,1024]{2,1,0:T(8,128)}, s32[]{:T(128)}, /*index=5*/s32[]{:T(128)...) while((s32[]{:T(128)}, f32[3,2048]{1,0:T(4,128)S(1)}, f32[9,2048]{1,0:T(8,128)}, ...), condition=%wide.region_8.9_spmd, body=%wide.region_6.8_spmd.sunk | while | flops 9673172992 | bytes 12929287 | solution.py:166
  344.3 12.4 %multiply_reduce_fusion.2 = f32[512,3]{0,1:T(4,128)S(1)} fusion(f32[512,1024]{1,0:T(8,128)S(1)} %select_add_fusion.12, f32[512,512,1]{0,1,2:T(8,128)S(1)} %bitcast.167, f32[3,512,1024]{2,1,0:T(8,128)} %get-tuple-element.681), kind=kOutput, calls=%fused_computation.2.clone.1 | convolution fusion | flops 9666820096 | bytes 9443328 | tf_op jit(solution)/shard_map/while/body/eval_jaxpr/sk,ckz->csz/dot_general | solution.py:162
  359.8 12.4 %multiply_reduce_fusion.2 = f32[512,3]{0,1:T(4,128)S(1)} fusion(f32[512,1024]{1,0:T(8,128)S(1)} %select_add_fusion.12, f32[512,512,1]{0,1,2:T(8,128)S(1)} %bitcast.167, f32[3,512,1024]{2,1,0:T(8,128)} %get-tuple-element.681), kind=kOutput, calls=%fused_computation.2.clone.1 | convolution fusion | flops 9666820096 | bytes 9443328 | tf_op jit(solution)/shard_map/while/body/eval_jaxpr/sk,ckz->csz/dot_general | solution.py:162
  375.4 12.4 %multiply_reduce_fusion.2 = f32[512,3]{0,1:T(4,128)S(1)} fusion(f32[512,1024]{1,0:T(8,128)S(1)} %select_add_fusion.12, f32[512,512,1]{0,1,2:T(8,128)S(1)} %bitcast.167, f32[3,512,1024]{2,1,0:T(8,128)} %get-tuple-element.681), kind=kOutput, calls=%fused_computation.2.clone.1 | convolution fusion | flops 9666820096 | bytes 9443328 | tf_op jit(solution)/shard_map/while/body/eval_jaxpr/sk,ckz->csz/dot_general | solution.py:162
  391.0 12.4 %multiply_reduce_fusion.2 = f32[512,3]{0,1:T(4,128)S(1)} fusion(f32[512,1024]{1,0:T(8,128)S(1)} %select_add_fusion.12, f32[512,512,1]{0,1,2:T(8,128)S(1)} %bitcast.167, f32[3,512,1024]{2,1,0:T(8,128)} %get-tuple-element.681), kind=kOutput, calls=%fused_computation.2.clone.1 | convolution fusion | flops 9666820096 | bytes 9443328 | tf_op jit(solution)/shard_map/while/body/eval_jaxpr/sk,ckz->csz/dot_general | solution.py:162
  404.6 8.5 %all-to-all-start.1 = ((f32[128,3,1,1,16]{4,3,2,1,0:T(1,128)}), f32[128,3,1,1,16]{4,3,2,1,0:T(1,128)S(1)}, u32[]{:S(2)}, u32[]{:S(2)}) async-start(f32[128,3,1,1,16]{4,3,2,1,0:T(1,128)} %reshape.1846), calls=%async_computation.1 | async-start | bytes 393216 | tf_op jit(solution)/shard_map/all_to_all | solution.py:27
  413.1 10.7 %all-to-all-done.1 = f32[128,3,1,1,16]{4,3,2,1,0:T(1,128)S(1)} async-done(((f32[128,3,1,1,16]{4,3,2,1,0:T(1,128)}), f32[128,3,1,1,16]{4,3,2,1,0:T(1,128)S(1)}, u32[]{:S(2)}, u32[]{:S(2)}) %all-to-all-start.1) | async-done | bytes 24608 | tf_op jit(solution)/shard_map/all_to_all | solution.py:27
  424.6 2.8 gather_fusion
  (205 shorter events, 67.8 us)
Async XLA Ops:
  13.0 22.3 %all-to-all-start = ((f32[128,1,144]{2,1,0:T(1,128)}), f32[128,1,144]{2,1,0:T(1,128)S(1)}, u32[]{:S(2)}, u32[]{:S(2)}) async-start(f32[128,1,144]{2,1,0:T(1,128)} %reshape.1849), calls=%async_computation | async-start | bytes 262144 | tf_op jit(solution)/shard_map/all_to_all | solution.py:27
  96.1 6.6 %copy-start.5 = (f32[9,2048]{1,0:T(8,128)}, f32[9,2048]{1,0:T(8,128)S(1)}, u32[]{:S(2)}) copy-start(f32[9,2048]{1,0:T(8,128)S(1)} %get-tuple-element.706) | copy-start | bytes 221188
  104.2 34.0 %collective-permute-start = (f32[3,2,32,1024]{3,2,1,0:T(8,128)S(1)}, f32[3,2,32,1024]{3,2,1,0:T(8,128)S(1)}, u32[]{:S(2)}, u32[]{:S(2)}) collective-permute-start(f32[3,2,32,1024]{3,2,1,0:T(8,128)S(1)} %get-tuple-element.427), channel_id=1, source_target_pairs={{0,16},{16,32},{32,48},{48,64},{64,80},{80,96},{96,112},{112,0},{1... | collective-permute-start | bytes 2359304 | tf_op jit(solution)/shard_map/ppermute | solution.py:38
  104.8 50.0 %slice-start = ((s8[6291456]{0:T(1024)(128)(4,1)}), s8[4194304]{0:T(1024)(128)(4,1)S(1)}, s32[]{:S(2)}) async-start(s8[6291456]{0:T(1024)(128)(4,1)} %bitcast.157), calls=%async_computation.2 | async-start | bytes 8388608
  104.8 40.0 %copy-start.1 = (f32[12,28,1024]{2,1,0:T(8,128)S(1)}, f32[12,28,1024]{2,1,0:T(8,128)}, u32[]{:S(2)}) copy-start(f32[12,28,1024]{2,1,0:T(8,128)} %param.11) | copy-start | bytes 4128772
  104.8 50.0 %slice-start.1 = ((s8[6291456]{0:T(1024)(128)(4,1)}), s8[2097152]{0:T(1024)(128)(4,1)S(1)}, s32[]{:S(2)}) async-start(s8[6291456]{0:T(1024)(128)(4,1)} %bitcast.157), calls=%async_computation.3 | async-start | bytes 4194304
  104.8 35.3 %collective-permute-start.1 = (f32[3,2,32,1024]{3,2,1,0:T(8,128)S(1)}, f32[3,2,32,1024]{3,2,1,0:T(8,128)S(1)}, u32[]{:S(2)}, u32[]{:S(2)}) collective-permute-start(f32[3,2,32,1024]{3,2,1,0:T(8,128)S(1)} %get-tuple-element.428), channel_id=1, source_target_pairs={{16,0},{32,16},{48,32},{64,48},{80,64},{96,80},{112,96},{0,112},{1... | collective-permute-start | bytes 2359304 | tf_op jit(solution)/shard_map/ppermute | solution.py:41
  142.6 8.6 %collective-permute-start.2 = (f32[3,20,2,1024]{3,1,2,0:T(8,128)S(1)}, f32[3,20,2,1024]{3,1,2,0:T(8,128)S(1)}, u32[]{:S(2)}, u32[]{:S(2)}) collective-permute-start(f32[3,20,2,1024]{3,1,2,0:T(8,128)S(1)} %copy.100), channel_id=1, source_target_pairs={{0,1},{1,2},{2,3},{3,4},{4,5},{5,6},{6,7},{7,8},{8,9},{9,10},{10,1... | collective-permute-start | bytes 1474568 | tf_op jit(solution)/shard_map/ppermute | solution.py:38
  144.6 9.8 %collective-permute-start.3 = (f32[3,20,2,1024]{3,1,2,0:T(8,128)S(1)}, f32[3,20,2,1024]{3,1,2,0:T(8,128)S(1)}, u32[]{:S(2)}, u32[]{:S(2)}) collective-permute-start(f32[3,20,2,1024]{3,1,2,0:T(8,128)S(1)} %copy.101), channel_id=1, source_target_pairs={{1,0},{2,1},{3,2},{4,3},{5,4},{6,5},{7,6},{8,7},{9,8},{10,9},{11,1... | collective-permute-start | bytes 1474568 | tf_op jit(solution)/shard_map/ppermute | solution.py:41
  164.1 16.8 %collective-permute-start.4 = (f32[3,1,28,1024]{3,2,1,0:T(8,128)S(1)}, f32[3,1,28,1024]{3,2,1,0:T(8,128)S(1)}, u32[]{:S(2)}, u32[]{:S(2)}) collective-permute-start(f32[3,1,28,1024]{3,2,1,0:T(8,128)S(1)} %get-tuple-element.456), channel_id=1, source_target_pairs={{16,0},{32,16},{48,32},{64,48},{80,64},{96,80},{112,96},{0,112},{1... | collective-permute-start | bytes 1032200 | tf_op jit(solution)/shard_map/ppermute | solution.py:41
  164.7 17.6 %collective-permute-start.5 = (f32[3,1,28,1024]{3,2,1,0:T(8,128)S(1)}, f32[3,1,28,1024]{3,2,1,0:T(8,128)S(1)}, u32[]{:S(2)}, u32[]{:S(2)}) collective-permute-start(f32[3,1,28,1024]{3,2,1,0:T(8,128)S(1)} %get-tuple-element.455), channel_id=1, source_target_pairs={{0,16},{16,32},{32,48},{48,64},{64,80},{80,96},{96,112},{112,0},{1... | collective-permute-start | bytes 1032200 | tf_op jit(solution)/shard_map/ppermute | solution.py:38
  182.4 7.3 %copy-start.4 = (f32[3,1,28,1024]{3,2,1,0:T(8,128)}, f32[3,1,28,1024]{3,2,1,0:T(8,128)S(1)}, u32[]{:S(2)}) copy-start(f32[3,1,28,1024]{3,2,1,0:T(8,128)S(1)} %collective-permute-done.5) | copy-start | bytes 1032196
  182.7 5.2 %collective-permute-start.6 = (f32[3,14,1,1024]{3,1,2,0:T(8,128)S(1)}, f32[3,14,1,1024]{3,1,2,0:T(8,128)S(1)}, u32[]{:S(2)}, u32[]{:S(2)}) collective-permute-start(f32[3,14,1,1024]{3,1,2,0:T(8,128)S(1)} %copy.104), channel_id=1, source_target_pairs={{1,0},{2,1},{3,2},{4,3},{5,4},{6,5},{7,6},{8,7},{9,8},{10,9},{11,1... | collective-permute-start | bytes 516104 | tf_op jit(solution)/shard_map/ppermute | solution.py:41
  184.7 4.1 collective-permute-start.7
  202.4 12.4 %collective-permute-start.8 = (f32[3,1,28,1024]{3,2,1,0:T(8,128)S(1)}, f32[3,1,28,1024]{3,2,1,0:T(8,128)S(1)}, u32[]{:S(2)}, u32[]{:S(2)}) collective-permute-start(f32[3,1,28,1024]{3,2,1,0:T(8,128)S(1)} %get-tuple-element.450), channel_id=1, source_target_pairs={{16,0},{32,16},{48,32},{64,48},{80,64},{96,80},{112,96},{0,112},{1... | collective-permute-start | bytes 1032200 | tf_op jit(solution)/shard_map/ppermute | solution.py:41
  205.8 16.4 %slice-start.4 = ((s8[4718592]{0:T(1024)(128)(4,1)}), s8[4194304]{0:T(1024)(128)(4,1)S(1)}, s32[]{:S(2)}) async-start(s8[4718592]{0:T(1024)(128)(4,1)} %bitcast.164), calls=%async_computation.6 | async-start | bytes 8388608
  205.8 16.4 %slice-start.5 = ((s8[4718592]{0:T(1024)(128)(4,1)}), s8[524288]{0:T(1024)(128)(4,1)S(1)}, s32[]{:S(2)}) async-start(s8[4718592]{0:T(1024)(128)(4,1)} %bitcast.164), calls=%async_computation.7 | async-start | bytes 1048576
  205.8 16.4 %collective-permute-start.9 = (f32[3,1,28,1024]{3,2,1,0:T(8,128)S(1)}, f32[3,1,28,1024]{3,2,1,0:T(8,128)S(1)}, u32[]{:S(2)}, u32[]{:S(2)}) collective-permute-start(f32[3,1,28,1024]{3,2,1,0:T(8,128)S(1)} %get-tuple-element.449), channel_id=1, source_target_pairs={{0,16},{16,32},{32,48},{48,64},{64,80},{80,96},{96,112},{112,0},{1... | collective-permute-start | bytes 1032200 | tf_op jit(solution)/shard_map/ppermute | solution.py:38
  222.1 7.2 %copy-start.3 = (f32[3,1,28,1024]{3,2,1,0:T(8,128)}, f32[3,1,28,1024]{3,2,1,0:T(8,128)S(1)}, u32[]{:S(2)}) copy-start(f32[3,1,28,1024]{3,2,1,0:T(8,128)S(1)} %collective-permute-done.9) | copy-start | bytes 1032196
  222.5 5.2 %collective-permute-start.10 = (f32[3,14,1,1024]{3,1,2,0:T(8,128)S(1)}, f32[3,14,1,1024]{3,1,2,0:T(8,128)S(1)}, u32[]{:S(2)}, u32[]{:S(2)}) collective-permute-start(f32[3,14,1,1024]{3,1,2,0:T(8,128)S(1)} %copy.108), channel_id=1, source_target_pairs={{1,0},{2,1},{3,2},{4,3},{5,4},{6,5},{7,6},{8,7},{9,8},{10,9},{11,1... | collective-permute-start | bytes 516104 | tf_op jit(solution)/shard_map/ppermute | solution.py:41
  224.1 4.4 %collective-permute-start.11 = (f32[3,14,1,1024]{3,1,2,0:T(8,128)S(1)}, f32[3,14,1,1024]{3,1,2,0:T(8,128)S(1)}, u32[]{:S(2)}, u32[]{:S(2)}) collective-permute-start(f32[3,14,1,1024]{3,1,2,0:T(8,128)S(1)} %copy.110), channel_id=1, source_target_pairs={{0,1},{1,2},{2,3},{3,4},{4,5},{5,6},{6,7},{7,8},{8,9},{9,10},{10,1... | collective-permute-start | bytes 516104 | tf_op jit(solution)/shard_map/ppermute | solution.py:38
  246.1 11.9 %collective-permute-start.12 = (f32[3,1,28,1024]{3,2,1,0:T(8,128)S(1)}, f32[3,1,28,1024]{3,2,1,0:T(8,128)S(1)}, u32[]{:S(2)}, u32[]{:S(2)}) collective-permute-start(f32[3,1,28,1024]{3,2,1,0:T(8,128)S(1)} %get-tuple-element.444), channel_id=1, source_target_pairs={{16,0},{32,16},{48,32},{64,48},{80,64},{96,80},{112,96},{0,112},{1... | collective-permute-start | bytes 1032200 | tf_op jit(solution)/shard_map/ppermute | solution.py:41
  248.6 15.7 %slice-start.2 = ((s8[4718592]{0:T(1024)(128)(4,1)}), s8[4194304]{0:T(1024)(128)(4,1)S(1)}, s32[]{:S(2)}) async-start(s8[4718592]{0:T(1024)(128)(4,1)} %bitcast.162), calls=%async_computation.4 | async-start | bytes 8388608
  248.6 15.7 %slice-start.3 = ((s8[4718592]{0:T(1024)(128)(4,1)}), s8[524288]{0:T(1024)(128)(4,1)S(1)}, s32[]{:S(2)}) async-start(s8[4718592]{0:T(1024)(128)(4,1)} %bitcast.162), calls=%async_computation.5 | async-start | bytes 1048576
  248.6 15.7 %collective-permute-start.13 = (f32[3,1,28,1024]{3,2,1,0:T(8,128)S(1)}, f32[3,1,28,1024]{3,2,1,0:T(8,128)S(1)}, u32[]{:S(2)}, u32[]{:S(2)}) collective-permute-start(f32[3,1,28,1024]{3,2,1,0:T(8,128)S(1)} %get-tuple-element.443), channel_id=1, source_target_pairs={{0,16},{16,32},{32,48},{48,64},{64,80},{80,96},{96,112},{112,0},{1... | collective-permute-start | bytes 1032200 | tf_op jit(solution)/shard_map/ppermute | solution.py:38
  264.3 8.9 %copy-start.2 = (f32[3,1,28,1024]{3,2,1,0:T(8,128)}, f32[3,1,28,1024]{3,2,1,0:T(8,128)S(1)}, u32[]{:S(2)}) copy-start(f32[3,1,28,1024]{3,2,1,0:T(8,128)S(1)} %collective-permute-done.13) | copy-start | bytes 1032196
  264.7 6.8 %collective-permute-start.14 = (f32[3,14,1,1024]{3,1,2,0:T(8,128)S(1)}, f32[3,14,1,1024]{3,1,2,0:T(8,128)S(1)}, u32[]{:S(2)}, u32[]{:S(2)}) collective-permute-start(f32[3,14,1,1024]{3,1,2,0:T(8,128)S(1)} %copy.112), channel_id=1, source_target_pairs={{1,0},{2,1},{3,2},{4,3},{5,4},{6,5},{7,6},{8,7},{9,8},{10,9},{11,1... | collective-permute-start | bytes 516104 | tf_op jit(solution)/shard_map/ppermute | solution.py:41
  267.4 5.0 %collective-permute-start.15 = (f32[3,14,1,1024]{3,1,2,0:T(8,128)S(1)}, f32[3,14,1,1024]{3,1,2,0:T(8,128)S(1)}, u32[]{:S(2)}, u32[]{:S(2)}) collective-permute-start(f32[3,14,1,1024]{3,1,2,0:T(8,128)S(1)} %copy.114), channel_id=1, source_target_pairs={{0,1},{1,2},{2,3},{3,4},{4,5},{5,6},{6,7},{7,8},{8,9},{9,10},{10,1... | collective-permute-start | bytes 516104 | tf_op jit(solution)/shard_map/ppermute | solution.py:38
  288.7 36.7 %copy-start = (f32[3,12,28,1024]{3,2,1,0:T(8,128)S(1)}, f32[3,12,28,1024]{3,2,1,0:T(8,128)}, u32[]{:S(2)}) copy-start(f32[3,12,28,1024]{3,2,1,0:T(8,128)} %fusion.31) | copy-start | bytes 12386308
  290.9 30.5 %collective-permute-start.16 = (f32[3,2,28,1024]{3,1,2,0:T(2,128)S(1)}, f32[3,2,28,1024]{3,1,2,0:T(2,128)S(1)}, u32[]{:S(2)}, u32[]{:S(2)}) collective-permute-start(f32[3,2,28,1024]{3,1,2,0:T(2,128)S(1)} %copy.116), channel_id=1, source_target_pairs={{0,16},{16,32},{32,48},{48,64},{64,80},{80,96},{96,112},{112,0},{1... | collective-permute-start | bytes 2064392 | tf_op jit(solution)/shard_map/ppermute | solution.py:38
  293.6 31.6 %collective-permute-start.17 = (f32[3,2,28,1024]{3,1,2,0:T(2,128)S(1)}, f32[3,2,28,1024]{3,1,2,0:T(2,128)S(1)}, u32[]{:S(2)}, u32[]{:S(2)}) collective-permute-start(f32[3,2,28,1024]{3,1,2,0:T(2,128)S(1)} %copy.117), channel_id=1, source_target_pairs={{16,0},{32,16},{48,32},{64,48},{80,64},{96,80},{112,96},{0,112},{1... | collective-permute-start | bytes 2064392 | tf_op jit(solution)/shard_map/ppermute | solution.py:41
  326.0 6.6 %collective-permute-start.18 = (f32[3,16,2,1024]{3,1,2,0:T(8,128)S(1)}, f32[3,16,2,1024]{3,1,2,0:T(8,128)S(1)}, u32[]{:S(2)}, u32[]{:S(2)}) collective-permute-start(f32[3,16,2,1024]{3,1,2,0:T(8,128)S(1)} %copy.120), channel_id=1, source_target_pairs={{0,1},{1,2},{2,3},{3,4},{4,5},{5,6},{6,7},{7,8},{8,9},{9,10},{10,1... | collective-permute-start | bytes 1179656 | tf_op jit(solution)/shard_map/ppermute | solution.py:38
  328.0 7.7 %collective-permute-start.19 = (f32[3,16,2,1024]{3,1,2,0:T(8,128)S(1)}, f32[3,16,2,1024]{3,1,2,0:T(8,128)S(1)}, u32[]{:S(2)}, u32[]{:S(2)}) collective-permute-start(f32[3,16,2,1024]{3,1,2,0:T(8,128)S(1)} %copy.121), channel_id=1, source_target_pairs={{1,0},{2,1},{3,2},{4,3},{5,4},{6,5},{7,6},{8,7},{9,8},{10,9},{11,1... | collective-permute-start | bytes 1179656 | tf_op jit(solution)/shard_map/ppermute | solution.py:41
  404.6 19.2 %all-to-all-start.1 = ((f32[128,3,1,1,16]{4,3,2,1,0:T(1,128)}), f32[128,3,1,1,16]{4,3,2,1,0:T(1,128)S(1)}, u32[]{:S(2)}, u32[]{:S(2)}) async-start(f32[128,3,1,1,16]{4,3,2,1,0:T(1,128)} %reshape.1846), calls=%async_computation.1 | async-start | bytes 393216 | tf_op jit(solution)/shard_map/all_to_all | solution.py:27
where the time goes:
time: 434 us; the launch traced here: 428 us
  waiting for transfers between devices  129 us (30%)
  matrix products  103 us (24%)
  other arithmetic  84.5 us (19%)
  local copies, waits for them, and re-layouts  63.5 us (15%)
  starting transfers between devices  47.5 us (11%)
    ppermute x10, waiting for transfers between devices, extended(): lax.ppermute(lax.slice_in_dim(block, block.shape[dim] - width, None, axis...  81 us
    dot_general x4, matrix products, spread_block(): jnp.einsum('sk,csz->ckz', planar, pushed, precision=lax.Precision.HIGHEST)  52 us
    dot_general x4, matrix products, sample_block(): jnp.einsum('sk,ckz->csz', planar, field_flat, precision=lax.Precision.HIG...  49.5 us
    div x3, other arithmetic, shards(): field = (rhs + viscosity * neighbour_sum(padded)) / (1.0 + 6.0 * viscosity)  42.7 us
    slice x6, local copies, waits for them, and re-layouts, neighbour_sum(): beside_all = beside_all + jnp.roll(inner, -1, 3) + jnp.roll(inner, 1, 3)  27.1 us
    ppermute x10, waiting for transfers between devices, extended(): lax.ppermute(lax.slice_in_dim(block, 0, width, axis=dim), axis, backward)  26.8 us
    all_to_all x2, waiting for transfers between devices, joined_exchange(): lax.all_to_all(pieces, axis, split_axis=0, concat_axis=0, tiled=True)  20.8 us
    all_to_all x2, starting transfers between devices, joined_exchange(): lax.all_to_all(pieces, axis, split_axis=0, concat_axis=0, tiled=True)  20.6 us
  transfers between devices with their start and end apart: 22, of which 17 were waited for; matrix products, arithmetic and copies ran while one was open for 8% of the time, Pallas kernels for 0%

commit v1 on v0

v1 whole, which is shorter than its diff:
```python
import functools

import jax
import jax.numpy as jnp
from jax import lax
from jax.experimental import pallas as pl
from jax.experimental.pallas import tpu as pltpu
from jax.sharding import PartitionSpec as P

F32 = jnp.float32
BF16 = jnp.bfloat16
I32 = jnp.int32
LIMIT = 60 * 1024 * 1024
CAP = 16
HALO = 3
PAD = 8
YE = 40


def split3(x):
    hi = x.astype(BF16).astype(F32)
    rest = x - hi
    mid = rest.astype(BF16).astype(F32)
    return hi, mid, rest - mid


def split2(x):
    hi = x.astype(BF16)
    return hi, (x - hi.astype(F32)).astype(BF16)


def nn(a, b):
    return lax.dot_general(a, b, (((1,), (0,)), ((), ())), preferred_element_type=F32)


def nt(a, b):
    return lax.dot_general(a, b, (((1,), (1,)), ((), ())), preferred_element_type=F32)


def tn(a, b):
    return lax.dot_general(a, b, (((0,), (0,)), ((), ())), preferred_element_type=F32)


def iota(shape, dim):
    return lax.broadcasted_iota(I32, shape, dim)


def vmem():
    return pl.BlockSpec(memory_space=pltpu.VMEM)


def smem():
    return pl.BlockSpec(memory_space=pltpu.SMEM)


def params():
    return pltpu.CompilerParams(vmem_limit_bytes=LIMIT)


def cost(flops, size):
    return pl.CostEstimate(flops=flops, bytes_accessed=size, transcendentals=0)


def pack_kernel(owner_ref, cells_ref, offsets_ref, forces_ref, out_ref, rank_ref):
    markers = owner_ref.shape[1]
    devices = out_ref.shape[0]
    owner = owner_ref[...]
    before = (iota((128, 128), 0) < iota((128, 128), 1)).astype(BF16)
    running = jnp.zeros((devices, 1), F32)
    ranks = []
    hots = []
    for g in range(markers // 128):
        hot = (iota((devices, 128), 0) == owner[:, g * 128 : (g + 1) * 128]).astype(F32)
        within = nn(hot.astype(BF16), before)
        ranks.append(jnp.sum(hot * (within + running), axis=0, keepdims=True))
        running = running + jnp.sum(hot, axis=1, keepdims=True)
        hots.append(hot.astype(BF16))
    rank = jnp.concatenate(ranks, axis=1).astype(I32)
    rank_ref[...] = rank
    onehot = jnp.concatenate(hots, axis=1)
    payload = jnp.concatenate(
        [
            cells_ref[...].astype(F32),
            offsets_ref[...],
            forces_ref[...],
            jnp.ones((1, markers), F32),
            jnp.zeros((6, markers), F32),
        ],
        axis=0,
    )
    parts = split3(payload)
    total = None
    for part in parts:
        rows = jnp.concatenate([jnp.where(rank == k, part, 0.0) for k in range(CAP)], axis=0)
        term = nt(onehot, rows.astype(BF16))
        total = term if total is None else total + term
    out_ref[...] = total


def pack(owner_row, cells, offsets, forces, devices):
    markers = owner_row.shape[1]
    return pl.pallas_call(
        pack_kernel,
        out_shape=(
            jax.ShapeDtypeStruct((devices, CAP * 16), F32),
            jax.ShapeDtypeStruct((1, markers), I32),
        ),
        in_specs=[vmem()] * 4,
        out_specs=(vmem(), vmem()),
        compiler_params=params(),
        cost_estimate=cost(4 * 10**8, 300_000),
        name="pack",
    )(owner_row, cells, offsets, forces)


def place_block(flat, start, count):
    return (flat == start + iota((count, flat.shape[1]), 0)).astype(F32).astype(BF16)


def sort_kernel(depth, rec_ref, list_ref, rank_ref, keys, pieces):
    devices = rec_ref.shape[0]
    slots = devices * CAP
    rec = rec_ref[...]
    flipped = rec.T
    empty = float(depth * 4096)

    def key_of(z, valid, index):
        low = jnp.where(z < 0.5, float(depth - 1), z - 1.0)
        return jnp.where(valid > 0.5, low * float(slots), empty) + index

    rows = []
    lane = iota((devices, 128), 1)
    for k in range(CAP):
        at = k * 16
        column = key_of(
            rec[:, at + 2 : at + 3],
            rec[:, at + 9 : at + 10],
            (iota((devices, 1), 0) + k * devices).astype(F32),
        )
        keys[k] = jnp.broadcast_to(column, (devices, devices))
        rows.append(
            key_of(
                flipped[at + 2 : at + 3, :],
                flipped[at + 9 : at + 10, :],
                (iota((1, devices), 1) + k * devices).astype(F32),
            )
        )
        half = rec[:, (k // 8) * 128 : (k // 8 + 1) * 128]
        turned = half if k % 8 == 0 else pltpu.roll(half, 128 - (k % 8) * 16, 1)
        hi, mid, lo = split3(turned)
        joined = jnp.where(
            lane < 16,
            hi,
            jnp.where(
                lane < 32, pltpu.roll(mid, 16, 1), jnp.where(lane < 48, pltpu.roll(lo, 32, 1), 0.0)
            ),
        )
        pieces[k * devices : (k + 1) * devices, :] = joined.astype(BF16)
    ranks = []
    for k in range(CAP):
        row = rows[k]

        def count(other, acc):
            return acc + jnp.where(keys[other] < row, 1.0, 0.0)

        acc = lax.fori_loop(0, CAP, count, jnp.zeros((devices, devices), F32))
        ranks.append(jnp.sum(acc, axis=0, keepdims=True).astype(I32))
    rank_ref[...] = jnp.concatenate(ranks, axis=0)
    flat = jnp.concatenate(ranks, axis=1)
    block = 256
    for b in range(slots // block):
        moved = nn(place_block(flat, b * block, block), pieces[...]).T
        rows = moved[0:16] + moved[16:32] + moved[32:48]
        z = rows[2:3]
        low = jnp.where(z < 0.5, float(depth - 1), z - 1.0)
        list_ref[:, b * block : (b + 1) * block] = jnp.where(
            iota((16, block), 0) == 2, low, rows
        )
    lanes = iota((1, 128), 1)
    meta = jnp.zeros((1, 128), F32)
    chunks = jnp.zeros((1, 1), F32)
    for c in range(slots // 128):
        low = list_ref[2:3, c * 128 : (c + 1) * 128]
        valid = list_ref[9:10, c * 128 : (c + 1) * 128] > 0.5
        first = jnp.min(
            jnp.where(valid, jnp.floor(low / 128.0), 1000.0), axis=1, keepdims=True
        )
        last = jnp.max(
            jnp.where(valid, jnp.floor((low + 3.0) / 128.0), -1.0), axis=1, keepdims=True
        )
        number = jnp.maximum(last - first + 1.0, 0.0)
        chunks = chunks + jnp.where(number > 0.5, 1.0, 0.0)
        meta = meta + jnp.where(lanes == c, first, 0.0) + jnp.where(lanes == 16 + c, number, 0.0)
    meta = meta + jnp.where(lanes == 32, chunks, 0.0)
    list_ref[10:11, 0:128] = meta


def sort(received, depth):
    devices = received.shape[0]
    slots = devices * CAP
    return pl.pallas_call(
        functools.partial(sort_kernel, depth),
        out_shape=(
            jax.ShapeDtypeStruct((16, slots), F32),
            jax.ShapeDtypeStruct((CAP, devices), I32),
        ),
        in_specs=[vmem()],
        out_specs=(vmem(), vmem()),
        scratch_shapes=[
            pltpu.VMEM((CAP, devices, devices), F32),
            pltpu.VMEM((slots, 128), BF16),
        ],
        compiler_params=params(),
        cost_estimate=cost(2 * 10**9, 300_000),
        name="sort",
    )(received)


def bump(frac):
    root = jnp.sqrt(1.0 + 4.0 * frac - 4.0 * frac * frac)
    return (
        (3.0 - 2.0 * frac - root) / 8.0,
        (3.0 - 2.0 * frac + root) / 8.0,
        (1.0 + 2.0 * frac + root) / 8.0,
        (1.0 + 2.0 * frac - root) / 8.0,
    )


def tent(first, weights, count, modulus=None):
    rows = iota((count, 128), 0)
    table = jnp.zeros((count, 128), F32)
    for i in range(4):
        table = table + jnp.where(rows == first + i, weights[i], 0.0)
    return table


def planar_of(ref, at, lanes, shift_x, rows_x, shift_y, rows_y):
    part = ref[at, :, lanes]
    x = part[0:1].astype(I32) + shift_x
    y = part[1:2].astype(I32) + shift_y
    table_x = tent(x, bump(part[3:4]), -(-rows_x // 8) * 8)
    table_y = tent(y, bump(part[4:5]), rows_y)
    planar = jnp.concatenate([table_x[r : r + 1] * table_y for r in range(rows_x)], axis=0)
    return part, planar


def window_of(low, weights, window, depth):
    rows = iota((128, 128), 0) + window * 128
    table = jnp.zeros((128, 128), F32)
    for i in range(4):
        target = jnp.bitwise_and(low + i, depth - 1)
        table = table + jnp.where(rows == target, weights[i], 0.0)
    return table


def spread_kernel(size_x, size_y, meta, mid_ref, low_ref, high_ref, out_ref):
    depth = out_ref.shape[3]
    windows = depth // 128

    def clear(e, carry):
        for c in range(3):
            out_ref[c, e] = jnp.zeros((YE, depth), F32)
        return carry

    lax.fori_loop(0, size_x + 2 * HALO, clear, 0)
    rows_of = {-1: (0, 6), 0: (2, 16), 1: (14, 4)}
    cols_of = {-1: (0, 16), 0: (0, YE), 1: (32, 8)}
    for dy, ref in ((0, mid_ref), (-1, low_ref), (1, high_ref)):
        for dx in (-1, 0, 1):
            index = (dy + 1) * 3 + dx + 1
            e0, rows = rows_of[dx]
            s0, cols = cols_of[dy]

            def chunk_step(chunk, carry):
                lanes = pl.ds(pl.multiple_of(chunk * 128, 128), 128)
                part, planar = planar_of(
                    ref,
                    dx + 1,
                    lanes,
                    HALO - 1 + size_x * dx - e0,
                    rows,
                    PAD - 1 + size_y * dy - s0,
                    cols,
                )
                hi, lo = split2(planar)
                left = jnp.concatenate([hi, lo, hi, lo], axis=1)
                low = part[2:3].astype(I32)
                weights = bump(part[5:6])
                first = meta[index, chunk]

                def window_step(turn, inner):
                    window = jnp.bitwise_and(first + turn, windows - 1)
                    table = window_of(low, weights, window, depth)
                    pushed = jnp.concatenate([table * part[6 + c : 7 + c] for c in range(3)], axis=0)
                    big, small = split2(pushed)
                    right = jnp.concatenate([big, big, small, small], axis=1)
                    sums = nt(left, right)
                    at = pl.ds(pl.multiple_of(window * 128, 128), 128)
                    for c in range(3):
                        for r in range(rows):
                            out_ref[c, e0 + r, s0 : s0 + cols, at] += sums[
                                r * cols : (r + 1) * cols, c * 128 : (c + 1) * 128
                            ]
                    return inner

                lax.fori_loop(0, meta[index, 16 + chunk], window_step, 0)
                return carry

            lax.fori_loop(0, meta[index, 32], chunk_step, 0)


def spread(meta, mid, low, high, size_x, size_y, depth):
    return pl.pallas_call(
        functools.partial(spread_kernel, size_x, size_y),
        out_shape=jax.ShapeDtypeStruct((3, size_x + 2 * HALO, YE, depth), F32),
        in_specs=[smem(), vmem(), vmem(), vmem()],
        out_specs=vmem(),
        compiler_params=params(),
        cost_estimate=cost(10**10, 10**7),
        name="spread",
    )(meta, mid, low, high)


def faces_kernel(vel_ref, visc_ref, x_up, x_down, y_up, y_down):
    size_x, size_y = visc_ref.shape[0], visc_ref.shape[1]
    for l in range(HALO):
        for c in range(3):
            r = c * HALO + l
            x_up[r * size_y : (r + 1) * size_y, :] = vel_ref[c, size_x - HALO + l]
            x_down[r * size_y : (r + 1) * size_y, :] = vel_ref[c, l]
    for l in range(HALO - 1):
        r = 3 * HALO + l
        x_up[r * size_y : (r + 1) * size_y, :] = visc_ref[size_x - HALO + 1 + l]
        x_down[r * size_y : (r + 1) * size_y, :] = visc_ref[l]
    for x in range(size_x):
        for c in range(3):
            r = (c * size_x + x) * HALO
            y_up[r : r + HALO, :] = vel_ref[c, x, size_y - HALO : size_y, :]
            y_down[r : r + HALO, :] = vel_ref[c, x, 0:HALO, :]
        r = 3 * size_x * HALO + x * (HALO - 1)
        y_up[r : r + HALO - 1, :] = visc_ref[x, size_y - HALO + 1 : size_y, :]
        y_down[r : r + HALO - 1, :] = visc_ref[x, 0 : HALO - 1, :]


X_LAYERS = 4 * HALO - 1


def face_rows(size_x, size_y):
    rows_x = X_LAYERS * size_y
    rows_y = 3 * size_x * HALO + size_x * (HALO - 1)
    return -(-rows_x // 8) * 8, -(-rows_y // 8) * 8


def faces(velocity, viscosity):
    size_x, size_y, depth = viscosity.shape
    rows_x, rows_y = face_rows(size_x, size_y)
    shape_x = jax.ShapeDtypeStruct((rows_x, depth), F32)
    shape_y = jax.ShapeDtypeStruct((rows_y, depth), F32)
    return pl.pallas_call(
        faces_kernel,
        out_shape=(shape_x, shape_x, shape_y, shape_y),
        in_specs=[vmem(), vmem()],
        out_specs=(vmem(),) * 4,
        compiler_params=params(),
        cost_estimate=cost(10**6, 10**7),
        name="faces",
    )(velocity, viscosity)


def corners_kernel(size_y, low_ref, high_ref, up, down):
    for side, ref in ((0, low_ref), (1, high_ref)):
        for r in range(X_LAYERS):
            at = (side * X_LAYERS + r) * HALO
            up[at : at + HALO, :] = ref[(r + 1) * size_y - HALO : (r + 1) * size_y, :]
            down[at : at + HALO, :] = ref[r * size_y : r * size_y + HALO, :]


def corners(low, high, size_y):
    rows = -(-2 * X_LAYERS * HALO // 8) * 8
    shape = jax.ShapeDtypeStruct((rows, low.shape[1]), F32)
    return pl.pallas_call(
        functools.partial(corners_kernel, size_y),
        out_shape=(shape, shape),
        in_specs=[vmem(), vmem()],
        out_specs=(vmem(), vmem()),
        compiler_params=params(),
        cost_estimate=cost(10**6, 3 * 10**6),
        name="corners",
    )(low, high)


def solve_kernel(
    sweeps,
    meta,
    spread_ref,
    vel_ref,
    visc_ref,
    x_low,
    x_high,
    y_low,
    y_high,
    c_low,
    c_high,
    mid_ref,
    low_ref,
    high_ref,
    new_ref,
    part_mid,
    part_low,
    part_high,
    rhs,
    scaled,
    field,
    ratio,
):
    size_x, size_y, depth = visc_ref.shape
    ext = size_x + 2 * HALO
    own = slice(PAD, PAD + size_y)
    below = slice(PAD - HALO, PAD)
    above = slice(PAD + size_y, PAD + size_y + HALO)

    def clear(e, carry):
        ratio[e] = jnp.zeros((YE, depth), F32)
        return carry

    lax.fori_loop(0, ext - 2, clear, 0)
    base = 3 * size_x * HALO
    thin = HALO - 1
    for x in range(size_x):
        e = x + HALO - 1
        ratio[e, own, :] = visc_ref[x]
        ratio[e, PAD - thin : PAD, :] = y_low[base + x * thin : base + (x + 1) * thin, :]
        ratio[e, PAD + size_y : PAD + size_y + thin, :] = y_high[
            base + x * thin : base + (x + 1) * thin, :
        ]
    for side, ref in ((0, x_low), (1, x_high)):
        for l in range(thin):
            e = l if side == 0 else size_x + HALO - 1 + l
            r = 3 * HALO + l
            at = (side * X_LAYERS + r) * HALO
            ratio[e, own, :] = ref[r * size_y : (r + 1) * size_y, :]
            ratio[e, below, :] = c_low[at : at + HALO, :]
            ratio[e, above, :] = c_high[at : at + HALO, :]

    def clear_rhs(e, carry):
        for c in range(3):
            rhs[c, e] = jnp.zeros((YE, depth), F32)
        return carry

    lax.fori_loop(0, ext, clear_rhs, 0)
    for c in range(3):
        for x in range(size_x):
            e = x + HALO
            r = (c * size_x + x) * HALO
            rhs[c, e, own, :] = vel_ref[c, x]
            rhs[c, e, below, :] = y_low[r : r + HALO, :]
            rhs[c, e, above, :] = y_high[r : r + HALO, :]
        for side, ref in ((0, x_low), (1, x_high)):
            for l in range(HALO):
                e = l if side == 0 else size_x + HALO + l
                r = c * HALO + l
                at = (side * X_LAYERS + r) * HALO
                rhs[c, e, own, :] = ref[r * size_y : (r + 1) * size_y, :]
                rhs[c, e, below, :] = c_low[at : at + HALO, :]
                rhs[c, e, above, :] = c_high[at : at + HALO, :]

    def edge(e, carry):
        for c in range(3):
            rhs[c, e] = rhs[c, e] + spread_ref[c, e]
        return carry

    edge(0, 0)
    edge(ext - 1, 0)

    def scale(e, carry):
        for s in range(YE // 8):
            rows = slice(s * 8, s * 8 + 8)
            nu = ratio[e - 1, rows, :]
            inverse = 1.0 / (1.0 + 6.0 * nu)
            ratio[e - 1, rows, :] = nu * inverse
            for c in range(3):
                value = rhs[c, e, rows, :] + spread_ref[c, e, rows, :]
                rhs[c, e, rows, :] = value
                scaled[c, e - 1, rows, :] = value * inverse
        return carry

    lax.fori_loop(1, ext - 1, scale, 0)

    def sweep(source, offset, target, target_offset, first, last, write):
        def row(e, carry):
            for c in range(3):
                here = source[c, e - offset]
                beside = source[c, e + 1 - offset] + source[c, e - 1 - offset]
                beside = beside + pltpu.roll(here, YE - 1, 0) + pltpu.roll(here, 1, 0)
                beside = beside + pltpu.roll(here, depth - 1, 1) + pltpu.roll(here, 1, 1)
                value = scaled[c, e - 1] + ratio[e - 1] * beside
                if write:
                    value = jnp.where(iota((YE, depth), 0) < PAD + size_y, value, 0.0)
                target[c, e - target_offset] = value
                if write:
                    new_ref[c, e - HALO] = value[own]
            return carry

        lax.fori_loop(first, last, row, 0)

    sweep(rhs, 0, field, 1, 1, ext - 1, False)
    sweep(field, 1, rhs, 0, 2, ext - 2, False)
    sweep(rhs, 0, field, 1, 3, ext - 3, True)

    rows_of = {-1: (0, 2), 0: (0, size_x), 1: (size_x - 2, 2)}
    cols_of = {-1: (8, 8), 0: (8, 32), 1: (32, 8)}
    windows = depth // 128
    for dy, ref, part_ref in (
        (0, mid_ref, part_mid),
        (-1, low_ref, part_low),
        (1, high_ref, part_high),
    ):
        part_ref[...] = jnp.zeros(part_ref.shape, F32)
        for dx in (-1, 0, 1):
            index = (dy + 1) * 3 + dx + 1
            e0, rows = rows_of[dx]
            s0, cols = cols_of[dy]

            def chunk_step(chunk, carry):
                lanes = pl.ds(pl.multiple_of(chunk * 128, 128), 128)
                part, planar = planar_of(
                    ref, dx + 1, lanes, size_x * dx - 1 - e0, rows, PAD - 1 + size_y * dy - s0, cols
                )
                right = jnp.concatenate(split2(planar), axis=1)
                low = part[2:3].astype(I32)
                weights = bump(part[5:6])
                first = meta[index, chunk]

                def window_step(turn, sums):
                    window = jnp.bitwise_and(first + turn, windows - 1)
                    table = window_of(low, weights, window, depth)
                    at = pl.ds(pl.multiple_of(window * 128, 128), 128)
                    new = []
                    for c in range(3):
                        values = jnp.concatenate(
                            [
                                field[c, e0 + HALO - 1 + r, s0 : s0 + cols, at]
                                for r in range(rows)
                            ],
                            axis=0,
                        )
                        big, small = split2(values)
                        got = tn(big, right) + tn(small, right)
                        got = got[:, 0:128] + got[:, 128:256]
                        new.append(sums[c] + jnp.sum(got * table, axis=0, keepdims=True))
                    return tuple(new)

                start = tuple(jnp.zeros((1, 128), F32) for _ in range(3))
                sums = lax.fori_loop(0, meta[index, 16 + chunk], window_step, start)
                for c in range(3):
                    at = (dx + 1) * 3 + c
                    part_ref[at : at + 1, lanes] = sums[c]
                return carry

            lax.fori_loop(0, meta[index, 32], chunk_step, 0)


def solve(sweeps, meta, spread_ext, velocity, viscosity, halos, lists):
    size_x, size_y, depth = viscosity.shape
    ext = size_x + 2 * HALO
    slots = lists[0].shape[2]
    partial = jax.ShapeDtypeStruct((9, slots), F32)
    return pl.pallas_call(
        functools.partial(solve_kernel, sweeps),
        out_shape=(jax.ShapeDtypeStruct(velocity.shape, F32), partial, partial, partial),
        in_specs=[smem()] + [vmem()] * 12,
        out_specs=(vmem(),) * 4,
        scratch_shapes=[
            pltpu.VMEM((3, ext, YE, depth), F32),
            pltpu.VMEM((3, ext - 2, YE, depth), F32),
            pltpu.VMEM((3, ext - 2, YE, depth), F32),
            pltpu.VMEM((ext - 2, YE, depth), F32),
        ],
        compiler_params=params(),
        cost_estimate=cost(10**10, 2 * 10**7),
        name="solve",
    )(meta, spread_ext, velocity, viscosity, *halos, *lists)


def unsort_kernel(total_ref, rank_ref, out_ref):
    devices = out_ref.shape[0]
    slots = total_ref.shape[1]
    flat = jnp.concatenate([rank_ref[k : k + 1, :] for k in range(CAP)], axis=1)
    block = 256
    sums = jnp.zeros((32, slots), F32)
    for b in range(slots // block):
        values = total_ref[:, b * block : (b + 1) * block]
        parts = jnp.concatenate([*split3(values), jnp.zeros_like(values)], axis=0)
        sums = sums + nn(parts.astype(BF16), place_block(flat, b * block, block))
    rows = sums[0:8] + sums[8:16] + sums[16:24]
    turned = jnp.concatenate(
        [rows[:, k * devices : (k + 1) * devices] for k in range(CAP)], axis=0
    )
    out_ref[...] = turned.T


def unsort(total, rank):
    devices = rank.shape[1]
    return pl.pallas_call(
        unsort_kernel,
        out_shape=jax.ShapeDtypeStruct((devices, CAP * 8), F32),
        in_specs=[vmem(), vmem()],
        out_specs=vmem(),
        compiler_params=params(),
        cost_estimate=cost(10**9, 300_000),
        name="unsort",
    )(total, rank)


def unpack_kernel(owner_ref, rank_ref, back_ref, out_ref):
    markers = owner_ref.shape[1]
    devices = back_ref.shape[0]
    onehot = (iota((devices, markers), 0) == owner_ref[...]).astype(F32).astype(BF16)
    rank = rank_ref[...]
    turned = back_ref[...].T
    picked = None
    for part in split3(turned):
        term = nn(part.astype(BF16), onehot)
        picked = term if picked is None else picked + term
    total = jnp.zeros((8, markers), F32)
    for k in range(CAP):
        total = total + jnp.where(rank == k, picked[k * 8 : (k + 1) * 8], 0.0)
    out_ref[...] = total[0:3]


def unpack(owner_row, rank, back):
    markers = owner_row.shape[1]
    return pl.pallas_call(
        unpack_kernel,
        out_shape=jax.ShapeDtypeStruct((3, markers), F32),
        in_specs=[vmem()] * 3,
        out_specs=vmem(),
        compiler_params=params(),
        cost_estimate=cost(10**8, 100_000),
        name="unpack",
    )(owner_row, rank, back)


def shift_up(x, axis):
    count = lax.axis_size(axis)
    return lax.ppermute(x, axis, [(i, (i + 1) % count) for i in range(count)])


def shift_down(x, axis):
    count = lax.axis_size(axis)
    return lax.ppermute(x, axis, [((i + 1) % count, i) for i in range(count)])


def shards(velocity, viscosity, cells, offsets, forces, owners):
    devices = lax.axis_size("gx") * lax.axis_size("gy")
    size_x, size_y, depth = viscosity.shape
    markers = owners.shape[0]
    owner_row = owners.reshape(1, markers)
    both = ("gx", "gy")

    x_up, x_down, y_up, y_down = faces(velocity, viscosity)
    x_low = shift_up(x_up, "gx")
    x_high = shift_down(x_down, "gx")
    y_low = shift_up(y_up, "gy")
    y_high = shift_down(y_down, "gy")

    outgoing, rank = pack(owner_row, cells, offsets, forces, devices)
    received = lax.all_to_all(outgoing, both, split_axis=0, concat_axis=0, tiled=True)
    markers_list, order = sort(received, depth)
    list_low = shift_up(markers_list, "gx")
    list_high = shift_down(markers_list, "gx")
    mid = jnp.stack([list_low, markers_list, list_high])
    low = shift_up(mid, "gy")
    high = shift_down(mid, "gy")
    meta = jnp.concatenate([part[:, 10, 0:64] for part in (low, mid, high)], axis=0).astype(I32)
    spread_ext = spread(meta, mid, low, high, size_x, size_y, depth)

    c_up, c_down = corners(x_low, x_high, size_y)
    c_low = shift_up(c_up, "gy")
    c_high = shift_down(c_down, "gy")
    halos = (x_low, x_high, y_low, y_high, c_low, c_high)
    field, part_mid, part_low, part_high = solve(
        3, meta, spread_ext, velocity, viscosity, halos, (mid, low, high)
    )
    part = part_mid + shift_down(part_low, "gy") + shift_up(part_high, "gy")
    total = part[3:6] + shift_down(part[0:3], "gx") + shift_up(part[6:9], "gx")
    total = jnp.pad(total, ((0, 5), (0, 0)))
    back = unsort(total, order)
    back = lax.all_to_all(back, both, split_axis=0, concat_axis=0, tiled=True)
    return (field, unpack(owner_row, rank, back))


def solution(mesh):
    in_specs = (
        P(None, "gx", "gy", None),
        P("gx", "gy", None),
        P(None, ("gx", "gy")),
        P(None, ("gx", "gy")),
        P(None, ("gx", "gy")),
        P(("gx", "gy"), None),
    )
    out_specs = (P(None, "gx", "gy", None), P(None, ("gx", "gy")))
    return jax.shard_map(shards, mesh=mesh, in_specs=in_specs, out_specs=out_specs, check_vma=False)
```

time: 434 us -> 307 us (0.71); the launches traced: 428 us -> 306 us
  Pallas kernels: 0 us -> 153 us
  matrix products: 103 us -> 0 us
  other arithmetic: 84.5 us -> 1.9 us
  waiting for transfers between devices: 129 us -> 70.3 us
  local copies, waits for them, and re-layouts: 63.5 us -> 8.97 us
  blocking collectives: 0 us -> 23.4 us
    pallas_call x0 -> x8, Pallas kernels: none -> 153 us  [the longest x1 74.8 us: solve(): pl.pallas_call(functools.partial(solve_kernel, sweeps), out_shape=(jax.Sh...]
    dot_general x9 -> x0, matrix products: 103 us -> none  [the longest x4 52 us: spread_block(): jnp.einsum('sk,csz->ckz', planar, pushed, precision=lax.Precision.HIGHEST)]
    div x27 -> x0, other arithmetic: 43 us -> none  [the longest x3 42.7 us: shards(): field = (rhs + viscosity * neighbour_sum(padded)) / (1.0 + 6.0 * viscosity)]
    ppermute x20 -> x14, waiting for transfers between devices: 108 us -> 68.8 us  [the longest x7 53.3 us: shift_down(): return lax.ppermute(x, axis, [((i + 1) % count, i) for i in range(count)])]
    slice x29 -> x2, local copies, waits for them, and re-layouts: 36.3 us -> 0.02 us  [the longest x1 0.01 us: shards(): total = part[3:6] + shift_down(part[0:3], 'gx') + shift_up(part[6:9], 'gx')]
    all_to_all x0 -> x1, blocking collectives: none -> 23.4 us  [shards(): back = lax.all_to_all(back, both, split_axis=0, concat_axis=0, tiled=True)]
    all_to_all x2 -> x1, waiting for transfers between devices: 20.8 us -> 1.53 us  [shards(): lax.all_to_all(outgoing, both, split_axis=0, concat_axis=0, tiled=True)]
    add x37 -> x2, other arithmetic: 18.3 us -> 0.95 us  [the longest x1 0.94 us: shards(): part = part_mid + shift_down(part_low, 'gy') + shift_up(part_high, 'gy')]
  transfers between devices with their start and end apart: 22 -> 15, of which waited for: 17 -> 7; matrix products, arithmetic and copies ran while one was open for 8% -> 1% of each run, Pallas kernels for 0% -> 23%
where the time goes in v1:
time: 307 us; the launch traced here: 306 us
  Pallas kernels  153 us (50%)
  waiting for transfers between devices  70.3 us (23%)
  starting transfers between devices  47.5 us (15%)
  blocking collectives  23.4 us (8%)
  local copies, waits for them, and re-layouts  8.97 us (3%)
    pallas_call x1, Pallas kernels, solve(): pl.pallas_call(functools.partial(solve_kernel, sweeps), out_shape=(jax.Sh...  74.8 us
    pallas_call x1, Pallas kernels, spread(): pl.pallas_call(functools.partial(spread_kernel, size_x, size_y), out_shap...  54.4 us
    ppermute x7, waiting for transfers between devices, shift_down(): return lax.ppermute(x, axis, [((i + 1) % count, i) for i in range(count)])  53.3 us
    ppermute x7, starting transfers between devices, shift_down(): return lax.ppermute(x, axis, [((i + 1) % count, i) for i in range(count)])  32.1 us
    all_to_all x1, blocking collectives, shards(): back = lax.all_to_all(back, both, split_axis=0, concat_axis=0, tiled=True)  23.4 us
    ppermute x7, waiting for transfers between devices, shift_up(): return lax.ppermute(x, axis, [(i, (i + 1) % count) for i in range(count)])  15.6 us
    all_to_all x1, starting transfers between devices, shards(): lax.all_to_all(outgoing, both, split_axis=0, concat_axis=0, tiled=True)  11.5 us
    pallas_call x1, Pallas kernels, sort(): pl.pallas_call(functools.partial(sort_kernel, depth), out_shape=(jax.Shap...  9.26 us
  transfers between devices with their start and end apart: 15, of which 7 were waited for; matrix products, arithmetic and copies ran while one was open for 1% of the time, Pallas kernels for 23%

profile of v1, /device:TPU:1, one launch (start us, length us, event | category | flops | bytes accessed | tf_op | source)
XLA Modules:
  0.0 306.1 jit_solution(2732386753126200753)
XLA Ops:
  0.6 2.3 pack.1
  2.9 1.7 copy.13
  4.6 11.5 %all-to-all-start = ((f32[128,1,256]{2,1,0:T(1,128)}), f32[128,1,256]{2,1,0:T(1,128)S(1)}, u32[]{:S(2)}, u32[]{:S(2)}) async-start(f32[128,1,256]{2,1,0:T(1,128)} %copy.13), calls=%async_computation | async-start | bytes 262144 | tf_op jit(solution)/shard_map/all_to_all | solution.py:668
  16.1 4.8 %faces.1 = (f32[312,1024]{1,0:T(8,128)}, f32[312,1024]{1,0:T(8,128)}, f32[136,1024]{1,0:T(8,128)}, f32[136,1024]{1,0:T(8,128)}) custom-call(f32[3,12,28,1024]{3,2,1,0:T(8,128)} %vel_ref.3, f32[12,28,1024]{2,1,0:T(8,128)} %visc_ref.3), custom_call_target="tpu_custom_call" | custom-call | flops 1000000 | bytes 10000000 | tf_op jit(solution)/shard_map/faces/pallas_call | solution.py:359
  20.9 1.5 collective-permute-start.4
  22.4 2.3 collective-permute-start.5
  24.7 1.5 all-to-all-done
  26.2 0.7 copy.24
  26.9 9.3 %sort.1 = (f32[16,2048]{1,0:T(8,128)}, s32[16,128]{1,0:T(8,128)}) custom-call(f32[128,256]{1,0:T(8,128)} %bitcast.16), custom_call_target="tpu_custom_call" | custom-call | flops 2000000000 | bytes 300000 | tf_op jit(solution)/shard_map/sort/pallas_call | solution.py:201
  36.1 1.1 collective-permute-start.1
  37.2 0.4 collective-permute-start
  37.6 1.0 stack.13
  38.6 46.1 %collective-permute-done.1 = f32[16,2048]{1,0:T(8,128)S(1)} collective-permute-done((f32[16,2048]{1,0:T(8,128)}, f32[16,2048]{1,0:T(8,128)S(1)}, u32[]{:S(2)}, u32[]{:S(2)}) %collective-permute-start.1) | collective-permute-done | bytes 131104 | tf_op jit(solution)/shard_map/ppermute | solution.py:651
  84.7 0.1 stack.14
  84.8 0.0 collective-permute-done
  84.8 0.1 stack.12
  84.9 0.3 pad_maximum_fusion
  85.3 0.2 copy.14.mid_ref
  85.5 1.4 collective-permute-start.3
  87.0 1.2 collective-permute-start.2
  88.1 0.4 collective-permute-start.6
  88.6 4.9 %collective-permute-done.3.high_ref = f32[3,16,2048]{2,1,0:T(8,128)S(1)} collective-permute-done((f32[3,16,2048]{2,1,0:T(8,128)S(1)}, f32[3,16,2048]{2,1,0:T(8,128)S(1)}, u32[]{:S(2)}, u32[]{:S(2)}) %collective-permute-start.3) | collective-permute-done | bytes 393248 | tf_op jit(solution)/shard_map/ppermute | solution.py:651
  93.5 2.8 collective-permute-start.7
  96.3 0.0 collective-permute-done.2
  96.3 1.0 copy.16.low_ref
  97.3 0.6 maximum_convert_fusion.meta
  97.9 0.0 collective-permute-done.5.high_ref.x_high
  97.9 1.0 copy-done
  98.9 1.1 copy-done.1
  100.0 2.7 corners.1
  102.7 0.4 collective-permute-start.8
  103.1 6.6 %collective-permute-start.9 = (f32[72,1024]{1,0:T(8,128)}, f32[72,1024]{1,0:T(8,128)S(1)}, u32[]{:S(2)}, u32[]{:S(2)}) collective-permute-start(f32[72,1024]{1,0:T(8,128)} %get-tuple-element.23), channel_id=1, source_target_pairs={{1,0},{2,1},{3,2},{4,3},{5,4},{6,5},{7,6},{8,7},{9,8},{10,9},{11,1... | collective-permute-start | bytes 884744 | tf_op jit(solution)/shard_map/ppermute | solution.py:651
  109.7 54.4 %spread.1.spread_ref = f32[3,18,40,1024]{3,2,1,0:T(8,128)} custom-call(s32[9,64]{1,0:T(8,128)} %maximum_convert_fusion.meta, f32[3,16,2048]{2,1,0:T(8,128)} %copy-done.2, f32[3,16,2048]{2,1,0:T(8,128)} %copy.16.low_ref, f32[3,16,2048]{2,1,0:T(8,128)} %copy-done.3), custom_call_target="tpu_custom_call" | custom-call | flops 10000000000 | bytes 10000000 | tf_op jit(solution)/shard_map/spread/pallas_call | solution.py:313
  164.1 0.0 collective-permute-done.6.y_low
  164.1 0.7 copy-done.5
  164.8 0.7 copy-done.6
  165.6 74.8 %solve.1 = (f32[3,12,28,1024]{3,2,1,0:T(8,128)}, f32[9,2048]{1,0:T(8,128)}, f32[9,2048]{1,0:T(8,128)}, f32[9,2048]{1,0:T(8,128)}) custom-call(s32[9,64]{1,0:T(8,128)} %maximum_convert_fusion.meta, f32[3,18,40,1024]{3,2,1,0:T(8,128)} %spread.1.spread_ref, f32[3,12,28,1024]{3,2,1,0:T(8,128)} %vel_ref.3, f32[12,28,1024]{2,1,0:T(8,128)} %visc_ref.3, ...), custom_call_target="tpu_custom_call" | custom-call | flops 10000000000 | bytes 20000000 | tf_op jit(solution)/shard_map/solve/pallas_call | solution.py:568
  240.3 13.9 %collective-permute-start.10 = (f32[9,2048]{1,0:T(8,128)}, f32[9,2048]{1,0:T(8,128)S(1)}, u32[]{:S(2)}, u32[]{:S(2)}) collective-permute-start(f32[9,2048]{1,0:T(8,128)} %get-tuple-element.27), channel_id=1, source_target_pairs={{1,0},{2,1},{3,2},{4,3},{5,4},{6,5},{7,6},{8,7},{9,8},{10,9},{11,1... | collective-permute-start | bytes 221192 | tf_op jit(solution)/shard_map/ppermute | solution.py:651
  254.2 1.2 collective-permute-done.10
  255.4 11.7 %collective-permute-done.11 = f32[9,2048]{1,0:T(8,128)S(1)} collective-permute-done((f32[9,2048]{1,0:T(8,128)}, f32[9,2048]{1,0:T(8,128)S(1)}, u32[]{:S(2)}, u32[]{:S(2)}) %collective-permute-start.11) | collective-permute-done | bytes 73760 | tf_op jit(solution)/shard_map/ppermute | solution.py:646
  267.1 0.9 add_add_fusion
  268.0 4.1 %collective-permute-start.12 = (f32[3,2048]{1,0:T(4,128)S(1)}, f32[3,2048]{1,0:T(4,128)S(1)}, u32[]{:S(2)}, u32[]{:S(2)}) collective-permute-start(f32[3,2048]{1,0:T(4,128)S(1)} %get-tuple-element.30), channel_id=1, source_target_pairs={{16,0},{32,16},{48,32},{64,48},{80,64},{96,80},{112,96},{0,112},{1... | collective-permute-start | bytes 73736 | tf_op jit(solution)/shard_map/ppermute | solution.py:651
  272.1 1.0 collective-permute-done.12
  273.1 3.9 %collective-permute-done.13 = f32[3,2048]{1,0:T(4,128)S(1)} collective-permute-done((f32[3,2048]{1,0:T(4,128)S(1)}, f32[3,2048]{1,0:T(4,128)S(1)}, u32[]{:S(2)}, u32[]{:S(2)}) %collective-permute-start.13) | collective-permute-done | bytes 24608 | tf_op jit(solution)/shard_map/ppermute | solution.py:646
  277.0 0.6 pad.4.total_ref
  277.7 3.1 %unsort.1 = f32[128,128]{1,0:T(8,128)} custom-call(f32[8,2048]{1,0:T(8,128)} %pad.4.total_ref, s32[16,128]{1,0:T(8,128)} %get-tuple-element.29.rank_ref), custom_call_target="tpu_custom_call" | custom-call | flops 1000000000 | bytes 300000 | tf_op jit(solution)/shard_map/unsort/pallas_call | solution.py:604
  280.8 23.4 %all_to_all.22 = f32[128,1,128]{2,1,0:T(1,128)} all-to-all(f32[128,1,128]{2,1,0:T(1,128)} %bitcast.19), channel_id=1, replica_groups=mesh['gx'=8,'gy'=16] {'gx','gy'}, dimensions={0} | all-to-all | bytes 131072 | tf_op jit(solution)/shard_map/all_to_all | solution.py:689
  304.2 1.9 unpack.1
  (22 shorter events, 0.1 us)
Async XLA Ops:
  4.6 21.7 %all-to-all-start = ((f32[128,1,256]{2,1,0:T(1,128)}), f32[128,1,256]{2,1,0:T(1,128)S(1)}, u32[]{:S(2)}, u32[]{:S(2)}) async-start(f32[128,1,256]{2,1,0:T(1,128)} %copy.13), calls=%async_computation | async-start | bytes 262144 | tf_op jit(solution)/shard_map/all_to_all | solution.py:668
  20.9 77.0 %collective-permute-start.4 = (f32[312,1024]{1,0:T(8,128)}, f32[312,1024]{1,0:T(8,128)S(1)}, u32[]{:S(2)}, u32[]{:S(2)}) collective-permute-start(f32[312,1024]{1,0:T(8,128)} %get-tuple-element.18), channel_id=1, source_target_pairs={{0,16},{16,32},{32,48},{48,64},{64,80},{80,96},{96,112},{112,0},{1... | collective-permute-start | bytes 3833864 | tf_op jit(solution)/shard_map/ppermute | solution.py:646
  22.4 75.5 %collective-permute-start.5 = (f32[312,1024]{1,0:T(8,128)}, f32[312,1024]{1,0:T(8,128)S(1)}, u32[]{:S(2)}, u32[]{:S(2)}) collective-permute-start(f32[312,1024]{1,0:T(8,128)} %get-tuple-element.19), channel_id=1, source_target_pairs={{16,0},{32,16},{48,32},{64,48},{80,64},{96,80},{112,96},{0,112},{1... | collective-permute-start | bytes 3833864 | tf_op jit(solution)/shard_map/ppermute | solution.py:651
  36.1 57.4 %copy-start.4 = (f32[136,1024]{1,0:T(8,128)S(1)}, f32[136,1024]{1,0:T(8,128)}, u32[]{:S(2)}) copy-start(f32[136,1024]{1,0:T(8,128)} %get-tuple-element.21) | copy-start | bytes 1671172
  36.1 48.6 %collective-permute-start.1 = (f32[16,2048]{1,0:T(8,128)}, f32[16,2048]{1,0:T(8,128)S(1)}, u32[]{:S(2)}, u32[]{:S(2)}) collective-permute-start(f32[16,2048]{1,0:T(8,128)} %get-tuple-element.17), channel_id=1, source_target_pairs={{16,0},{32,16},{48,32},{64,48},{80,64},{96,80},{112,96},{0,112},{1... | collective-permute-start | bytes 393224 | tf_op jit(solution)/shard_map/ppermute | solution.py:651
  37.2 47.6 %collective-permute-start = (f32[16,2048]{1,0:T(8,128)}, f32[16,2048]{1,0:T(8,128)S(1)}, u32[]{:S(2)}, u32[]{:S(2)}) collective-permute-start(f32[16,2048]{1,0:T(8,128)} %get-tuple-element.17), channel_id=1, source_target_pairs={{0,16},{16,32},{32,48},{48,64},{64,80},{80,96},{96,112},{112,0},{1... | collective-permute-start | bytes 393224 | tf_op jit(solution)/shard_map/ppermute | solution.py:646
  85.5 17.2 %copy-start.2 = (f32[3,16,2048]{2,1,0:T(8,128)}, f32[3,16,2048]{2,1,0:T(8,128)S(1)}, u32[]{:S(2)}) copy-start(f32[3,16,2048]{2,1,0:T(8,128)S(1)} %copy.14.mid_ref) | copy-start | bytes 1179652
  85.5 8.0 %collective-permute-start.3 = (f32[3,16,2048]{2,1,0:T(8,128)S(1)}, f32[3,16,2048]{2,1,0:T(8,128)S(1)}, u32[]{:S(2)}, u32[]{:S(2)}) collective-permute-start(f32[3,16,2048]{2,1,0:T(8,128)S(1)} %copy.14.mid_ref), channel_id=1, source_target_pairs={{1,0},{2,1},{3,2},{4,3},{5,4},{6,5},{7,6},{8,7},{9,8},{10,9},{11,1... | collective-permute-start | bytes 1179656 | tf_op jit(solution)/shard_map/ppermute | solution.py:651
  87.0 9.3 %collective-permute-start.2 = (f32[3,16,2048]{2,0,1:T(4,128)S(1)}, f32[3,16,2048]{2,0,1:T(4,128)S(1)}, u32[]{:S(2)}, u32[]{:S(2)}) collective-permute-start(f32[3,16,2048]{2,0,1:T(4,128)S(1)} %pad_maximum_fusion), channel_id=1, source_target_pairs={{0,1},{1,2},{2,3},{3,4},{4,5},{5,6},{6,7},{7,8},{8,9},{9,10},{10,1... | collective-permute-start | bytes 1179656 | tf_op jit(solution)/shard_map/ppermute | solution.py:646
  88.1 76.0 %collective-permute-start.6 = (f32[136,1024]{1,0:T(8,128)}, f32[136,1024]{1,0:T(8,128)}, u32[]{:S(2)}, u32[]{:S(2)}) collective-permute-start(f32[136,1024]{1,0:T(8,128)} %get-tuple-element.20), channel_id=1, source_target_pairs={{0,1},{1,2},{2,3},{3,4},{4,5},{5,6},{6,7},{7,8},{8,9},{9,10},{10,1... | collective-permute-start | bytes 1671176 | tf_op jit(solution)/shard_map/ppermute | solution.py:646
  93.5 9.2 %copy-start.3 = (f32[3,16,2048]{2,1,0:T(8,128)}, f32[3,16,2048]{2,1,0:T(8,128)S(1)}, u32[]{:S(2)}) copy-start(f32[3,16,2048]{2,1,0:T(8,128)S(1)} %collective-permute-done.3.high_ref) | copy-start | bytes 1179652
  93.5 70.6 %collective-permute-start.7 = (f32[136,1024]{1,0:T(8,128)S(1)}, f32[136,1024]{1,0:T(8,128)}, u32[]{:S(2)}, u32[]{:S(2)}) collective-permute-start(f32[136,1024]{1,0:T(8,128)S(1)} %copy-done.4), channel_id=1, source_target_pairs={{1,0},{2,1},{3,2},{4,3},{5,4},{6,5},{7,6},{8,7},{9,8},{10,9},{11,1... | collective-permute-start | bytes 1671176 | tf_op jit(solution)/shard_map/ppermute | solution.py:651
  97.9 1.0 copy-start
  98.9 1.1 copy-start.1
  102.7 61.4 %collective-permute-start.8 = (f32[72,1024]{1,0:T(8,128)}, f32[72,1024]{1,0:T(8,128)S(1)}, u32[]{:S(2)}, u32[]{:S(2)}) collective-permute-start(f32[72,1024]{1,0:T(8,128)} %get-tuple-element.22), channel_id=1, source_target_pairs={{0,1},{1,2},{2,3},{3,4},{4,5},{5,6},{6,7},{7,8},{8,9},{9,10},{10,1... | collective-permute-start | bytes 884744 | tf_op jit(solution)/shard_map/ppermute | solution.py:646
  103.1 61.0 %collective-permute-start.9 = (f32[72,1024]{1,0:T(8,128)}, f32[72,1024]{1,0:T(8,128)S(1)}, u32[]{:S(2)}, u32[]{:S(2)}) collective-permute-start(f32[72,1024]{1,0:T(8,128)} %get-tuple-element.23), channel_id=1, source_target_pairs={{1,0},{2,1},{3,2},{4,3},{5,4},{6,5},{7,6},{8,7},{9,8},{10,9},{11,1... | collective-permute-start | bytes 884744 | tf_op jit(solution)/shard_map/ppermute | solution.py:651
  164.1 0.7 copy-start.5
  164.8 0.7 copy-start.6
  240.3 15.1 %collective-permute-start.10 = (f32[9,2048]{1,0:T(8,128)}, f32[9,2048]{1,0:T(8,128)S(1)}, u32[]{:S(2)}, u32[]{:S(2)}) collective-permute-start(f32[9,2048]{1,0:T(8,128)} %get-tuple-element.27), channel_id=1, source_target_pairs={{1,0},{2,1},{3,2},{4,3},{5,4},{6,5},{7,6},{8,7},{9,8},{10,9},{11,1... | collective-permute-start | bytes 221192 | tf_op jit(solution)/shard_map/ppermute | solution.py:651
  254.2 12.9 %collective-permute-start.11 = (f32[9,2048]{1,0:T(8,128)}, f32[9,2048]{1,0:T(8,128)S(1)}, u32[]{:S(2)}, u32[]{:S(2)}) collective-permute-start(f32[9,2048]{1,0:T(8,128)} %get-tuple-element.28), channel_id=1, source_target_pairs={{0,1},{1,2},{2,3},{3,4},{4,5},{5,6},{6,7},{7,8},{8,9},{9,10},{10,1... | collective-permute-start | bytes 221192 | tf_op jit(solution)/shard_map/ppermute | solution.py:646
  268.0 5.1 %collective-permute-start.12 = (f32[3,2048]{1,0:T(4,128)S(1)}, f32[3,2048]{1,0:T(4,128)S(1)}, u32[]{:S(2)}, u32[]{:S(2)}) collective-permute-start(f32[3,2048]{1,0:T(4,128)S(1)} %get-tuple-element.30), channel_id=1, source_target_pairs={{16,0},{32,16},{48,32},{64,48},{80,64},{96,80},{112,96},{0,112},{1... | collective-permute-start | bytes 73736 | tf_op jit(solution)/shard_map/ppermute | solution.py:651
  272.1 4.9 %collective-permute-start.13 = (f32[3,2048]{1,0:T(4,128)S(1)}, f32[3,2048]{1,0:T(4,128)S(1)}, u32[]{:S(2)}, u32[]{:S(2)}) collective-permute-start(f32[3,2048]{1,0:T(4,128)S(1)} %get-tuple-element.31), channel_id=1, source_target_pairs={{0,16},{16,32},{32,48},{48,64},{64,80},{80,96},{96,112},{112,0},{1... | collective-permute-start | bytes 73736 | tf_op jit(solution)/shard_map/ppermute | solution.py:646
